TPU v7x, 32 devices: a whole 2x2x4 slice. The times are simulated.
32 devices in a mesh: members: 2 (over y), gx: 16 (over z, x, core).
Axes of the slice: x: 2, y: 2, z: 4, core: 2. Of those that a mesh axis runs over, the one named last changes fastest.
Arguments:
- pressure: float32 [64, 32, 128], P(('members', 'gx')), parts along dimension 0, may hold values from -6 to 6
- saturation: float32 [64, 32, 128], P(('members', 'gx')), parts along dimension 0, may hold values from 0.1 to 0.9
- lam_water: float32 [64, 32, 128], P(('members', 'gx')), parts along dimension 0, may hold values from -6 to 6
- lam_oil: float32 [64, 32, 128], P(('members', 'gx')), parts along dimension 0, may hold values from -6 to 6
- perm_x: float32 [64, 32, 128], P(('members', 'gx')), parts along dimension 0, may hold values from 0.1 to 10
- perm_y: float32 [64, 32, 128], P(('members', 'gx')), parts along dimension 0, may hold values from 0.1 to 10
- perm_z: float32 [64, 32, 128], P(('members', 'gx')), parts along dimension 0, may hold values from 0.05 to 2
- pore_volume: float32 [64, 32, 128], P(('members', 'gx')), parts along dimension 0, may hold values from 0.3 to 3
- perf_cell: int32 [8192], P(('members', 'gx')), parts along dimension 0, may hold values from 0 to 8191
- perf_well: int32 [8192], P(('members', 'gx')), parts along dimension 0, may hold values from 0 to 255
- well_index: float32 [8192], P(('members', 'gx')), parts along dimension 0, may hold values from 0.5 to 5
- well_pressure: float32 [512], P(('members', 'gx')), parts along dimension 0, may hold values from -6 to 6
Outputs:
- grad_sat: float32 [64, 32, 128], P(('members', 'gx')), parts along dimension 0
- grad_bhp: float32 [512], P(('members', 'gx')), parts along dimension 0
- pressure_adj: float32 [64, 128, 32], P(('members', 'gx')), parts along dimension 0
There are 2 independent parts, one for each index of `members`. A program takes and returns all parts, laid end to end along the dimension named above; each array names one. Nothing has to cross between parts.
Inputs may be any that keep to these rules, and one draw needn't show every extreme that they name: `perf_cell`: perforation r lies in the box of device r // 256; the number counts cells of that box with x slowest and z fastest.
All inputs are finite; a program needn't handle non-finite values.
Results may differ from a plain program's by a relative error of at most 0.0001.
Values sent between devices are 32-bit elements; how exact they have to be, the bound alone decides.
No kernel may reach another device: no remote copies, remote signals or barrier semaphores. Data moves between devices by JAX's collectives and lax.ppermute only.
A program may use at most 64 MiB of HBM per device.

v0:
```python
import functools

import jax
import jax.numpy as jnp
from jax import lax
from jax.experimental import pallas as pl
from jax.experimental.pallas import tpu as pltpu
from jax.sharding import PartitionSpec as P

water_viscosity = 0.5
oil_viscosity = 2.0
compressibility = 0.2

LANES = 128
TILE = 8
RHS, DIAG, CY, CZ = (TILE * i for i in range(4))
LINKS = 4 * TILE
FACE = 5 * TILE
CY_BELOW = FACE + 4
WELL_ROW = FACE + 6
CHUNK = 6 * TILE


def mobilities(s):
    return s * s * (1.0 / water_viscosity), (1.0 - s) * (1.0 - s) * (1.0 / oil_viscosity)


def slopes(s):
    return s * (2.0 / water_viscosity), (s - 1.0) * (2.0 / oil_viscosity)


def split(x):
    first = x.astype(jnp.bfloat16)
    rest = x - first.astype(jnp.float32)
    second = rest.astype(jnp.bfloat16)
    third = (rest - second.astype(jnp.float32)).astype(jnp.bfloat16)
    return first, second, third


def dot(a, b, over):
    return lax.dot_general(a, b, (over, ((), ())), preferred_element_type=jnp.float32)


def add_thirds(x):
    n = x.shape[0] // 3
    return x[:n] + x[n : 2 * n] + x[2 * n :]


def marks(index, count):
    return (lax.broadcasted_iota(jnp.int32, (count, index.shape[1]), 0) == index).astype(jnp.float32)


def scatter_cells(values, row_marks, lane_marks):
    left = jnp.concatenate([(row_marks * part.astype(jnp.float32)).astype(jnp.bfloat16) for part in split(values)])
    return add_thirds(dot(left, lane_marks.astype(jnp.bfloat16), ((1,), (1,))))


def upper(x, axis):
    return pltpu.roll(x, x.shape[axis] - 1, axis)


def lower(x, axis):
    return pltpu.roll(x, 1, axis)


def transmissibility(k, axis):
    kn = upper(k, axis)
    at = lax.broadcasted_iota(jnp.int32, k.shape, axis)
    return jnp.where(at < k.shape[axis] - 1, 2.0 * k * kn / (k + kn), 0.0)


def load_kernel(*refs):
    count = (len(refs) - 2) // 2
    fields, loaded, edge, sems = refs[:count], refs[count : 2 * count], refs[-2], refs[-1]
    pairs = [(fields[f].at[1], edge.at[m]) for m, f in enumerate(range(5))] + list(zip(fields, loaded))
    copies = [pltpu.make_async_copy(src, dst, sems.at[i]) for i, (src, dst) in enumerate(pairs)]
    for copy in copies:
        copy.start()
    for copy in copies:
        copy.wait()


def face(here, there, trans):
    lw, lo, mw, mo = here
    lwn, lon, mwn, mon = there
    fw = mw + mwn
    fo = mo + mon
    return trans * (fw * (lw - lwn) + fo * (lo - lon)), trans * (fw + fo)


def cell_kernel(
    groups, sat, lamw, lamo, permx, permy, permz, pore, cell, well, index, bhp,
    rhs_out, diag_out, cy_out, cz_out, inner_out, weight, well_rows,
):
    ny = sat.shape[1]
    cells = cell[...]
    row_marks = marks(cells // LANES, 2 * ny)
    lane_marks = marks(cells % LANES, LANES)
    perf_weight = scatter_cells(index[...], row_marks, lane_marks)
    weight[...] = perf_weight
    flows, layers, rhs, diag = [], [], [], []
    for x in range(2):
        s, lw, lo = sat[x], lamw[x], lamo[x]
        mw, mo = mobilities(s)
        layers.append((lw, lo, mw, mo))
        flow = mw * lw + mo * lo
        flows.append(flow)
        w = perf_weight[x * ny : (x + 1) * ny]
        rhs.append(flow * w)
        diag.append(compressibility * pore[x] + (mw + mo) * w)
        for k, axis, out in ((permy[x], 0, cy_out), (permz[x], 1, cz_out)):
            there = tuple(upper(f, axis) for f in layers[x])
            g, c = face(layers[x], there, 0.5 * transmissibility(k, axis))
            rhs[x] += g - lower(g, axis)
            diag[x] += c + lower(c, axis)
            out[x] = c
    k, kn = permx[0], permx[1]
    g, c = face(layers[0], layers[1], k * kn / (k + kn))
    inner_out[...] = c
    for x in range(2):
        rhs_out[x] = rhs[x] + (1 - 2 * x) * g
        diag_out[x] = diag[x] + c

    flow_parts = jnp.concatenate(split(jnp.concatenate(flows)))
    row_parts = jnp.concatenate([row_marks.astype(jnp.bfloat16)] * 3)
    by_lane = dot(flow_parts, row_parts, ((0,), (0,)))
    inflow = index[...] * jnp.sum(by_lane * lane_marks, axis=0, keepdims=True)
    wells_each = bhp.shape[1]
    owners = marks(well[...] // wells_each, groups)
    places = marks(well[...] % wells_each + wells_each, LANES)
    well_rows[...] = scatter_cells(inflow, owners, places)
    well_rows[:, :wells_each] = jnp.broadcast_to(bhp[...], (groups, wells_each))


def pack_kernel(
    groups, press, sat, lamw, lamo, permx, from_below, rhs, diag, cy, cz, inner, well_rows,
    packed, sat_face, padded, padded_links,
):
    ny = sat.shape[1]
    k, kn = permx[0], from_below[4]
    trans = k * kn / (k + kn)
    lw, lo, lwn, lon = lamw[0], lamo[0], from_below[2], from_below[3]
    g, c = face((lw, lo, *mobilities(sat[0])), (lwn, lon, *mobilities(from_below[1])), trans)
    t = trans * (press[0] - from_below[0])
    sat_face[0] = t * (lw - lwn)
    sat_face[1] = t * (lo - lon)

    def pad(ref, at, value, outside):
        edge = jnp.full((TILE, LANES), outside, jnp.float32)
        ref[(*at, slice(0, TILE))] = edge
        ref[(*at, slice(TILE, TILE + ny))] = value
        ref[(*at, slice(TILE + ny, 2 * TILE + ny))] = edge

    for x in range(2):
        pad(padded, (0, x), rhs[x] + g if x == 0 else rhs[x], 0.0)
        pad(padded, (1, x), diag[x] + c if x == 0 else diag[x], 1.0)
        pad(padded, (2, x), cy[x], 0.0)
        pad(padded, (3, x), cz[x], 0.0)
    for i, value in enumerate((inner[...], c, g)):
        pad(padded_links, (i,), value, 0.0)

    def chunk(d, _):
        start = TILE + 2 * d - 1
        for f, at in enumerate((RHS, DIAG, CY, CZ)):
            for x in range(2):
                packed[d, at + 4 * x : at + 4 * x + 4] = padded[f, x, pl.ds(start, 4)]
        for i, at in enumerate((LINKS, LINKS + 4, FACE)):
            packed[d, at : at + 4] = padded_links[i, pl.ds(start, 4)]
        for x in range(2):
            packed[d, CY_BELOW + x : CY_BELOW + x + 1] = padded[2, x, pl.ds(start - 1, 1)]
        packed[d, WELL_ROW : WELL_ROW + 1] = well_rows[pl.ds(d, 1)]
        packed[d, WELL_ROW + 1 : WELL_ROW + 2] = jnp.zeros((1, LANES), jnp.float32)
        return 0

    if groups <= 16:
        for d in range(groups):
            chunk(d, 0)
    else:
        lax.fori_loop(0, groups, chunk, 0)


def sat_kernel(press, sat, lamw, lamo, permx, permy, permz, pore, weight, sat_face, from_below, out, back):
    ny = sat.shape[1]

    def parts(here, there, trans):
        p, lw, lo = here
        pn, lwn, lon = there
        t = trans * (p - pn)
        return t * (lw - lwn), t * (lo - lon)

    layers = [tuple(r[x] for r in (press, lamw, lamo)) for x in range(2)]
    k, kn = permx[0], permx[1]
    inner = parts(layers[0], layers[1], k * kn / (k + kn))
    outer = (sat_face[0], sat_face[1])
    dw, do = slopes(from_below[1])
    back[...] = dw * outer[0] + do * outer[1]
    for x in range(2):
        p, lw, lo = layers[x]
        water, oil = (i + o for i, o in zip(inner, outer)) if x == 0 else inner
        for k, axis in ((permy[x], 0), (permz[x], 1)):
            there = tuple(upper(f, axis) for f in layers[x])
            a, b = parts(layers[x], there, 0.5 * transmissibility(k, axis))
            water = water + a + lower(a, axis)
            oil = oil + b + lower(b, axis)
        dw, do = slopes(sat[x])
        well = weight[x * ny : (x + 1) * ny] * p
        out[x] = pore[x] * (lw - lo) + dw * (water + well * lw) + do * (oil + well * lo)


def well_kernel(partial, from_above, sat, lamw, lamo, cell, well, index, well_rows, out, grad_bhp):
    ny = sat.shape[1]
    groups = well_rows.shape[0]
    wells_each = grad_bhp.shape[1]
    rows = well_rows[...]
    place = well[...] % wells_each
    owners = marks(well[...] // wells_each, groups)
    by_owner = add_thirds(
        dot(jnp.concatenate(split(rows)), marks(place, LANES).astype(jnp.bfloat16), ((1,), (0,)))
    )
    pressure = jnp.sum(by_owner * owners, axis=0, keepdims=True)
    cells = cell[...]
    drop = scatter_cells(index[...] * pressure, marks(cells // LANES, 2 * ny), marks(cells % LANES, LANES))
    for x in range(2):
        dw, do = slopes(sat[x])
        before = partial[x] if x == 0 else partial[x] + from_above[...]
        out[x] = before - (dw * lamw[x] + do * lamo[x]) * drop[x * ny : (x + 1) * ny]
    total = -jnp.sum(rows, axis=0, keepdims=True)
    grad_bhp[...] = total[:, wells_each : 2 * wells_each]


def swap(x):
    return pltpu.roll(x, 4, 0)


def sublane():
    return lax.broadcasted_iota(jnp.int32, (TILE, LANES), 0)


def sweep(targets, weights, inverses, middle):
    steps = len(targets)
    b = [targets[0]]
    for j in range(1, steps):
        b.append(targets[j] + weights[j - 1] * b[j - 1])
    diag_swapped, coupling, inverse = middle
    u = (b[-1] * diag_swapped + coupling * swap(b[-1])) * inverse
    found = [u]
    for j in range(steps - 2, -1, -1):
        u = inverses[j] * b[j] + weights[j] * u
        found.append(u)
    return found[::-1]


def first_kernel(received, rhs_out, cy_out, cyl_out, cz_out, weight_out, inverse_out, middle_out, u_out, send, well_rows):
    groups = received.shape[0]
    steps = groups
    low = sublane() < 4

    def tile(s, at):
        return received[s, at : at + TILE]

    none = jnp.zeros((TILE, LANES), jnp.float32)
    row = sublane() % 4
    links = [tile(s, LINKS) for s in range(groups)]
    swapped = [swap(t) for t in links]
    rhs, diag, cyl = [], [], []
    for s in range(groups):
        g = swap(tile(s + 1, FACE)) if s < groups - 1 else none
        c = links[s + 1] if s < groups - 1 else none
        rhs.append(tile(s, RHS) - jnp.where(low, 0.0, g))
        diag.append(tile(s, DIAG) + jnp.where(low, 0.0, c))
    cy = [tile(s, CY) for s in range(groups)]
    cz = [tile(s, CZ) for s in range(groups)]
    for s in range(groups):
        first = received[s, CY_BELOW : CY_BELOW + 1]
        second = received[s, CY_BELOW + 1 : CY_BELOW + 2]
        cyl.append(jnp.where(row == 0, jnp.where(low, first, second), lower(cy[s], 0)))

    def paired(tiles):
        out = []
        for s in range(groups // 2):
            here, mirror = tiles[s], tiles[groups - 1 - s]
            out.append(jnp.where(low, here, mirror))
            out.append(swap(jnp.where(low, mirror, here)))
        return out

    rhs, diag, cy, cyl, cz = (paired(tiles) for tiles in (rhs, diag, cy, cyl, cz))
    link = []
    for s in range(groups // 2):
        link.append(jnp.where(low, links[s], swapped[groups - 1 - s]))
        link.append(jnp.where(low, swapped[s + 1], links[groups - 1 - s]))
    weights, inverses = [], []
    d = diag[0]
    for j in range(steps - 1):
        inverse = 1.0 / d
        inverses.append(inverse)
        weights.append(link[j] * inverse)
        d = diag[j + 1] - link[j] * weights[j]
    d_swapped = swap(d)
    middle = (d_swapped, link[-1], 1.0 / (d * d_swapped - link[-1] * link[-1]))

    u = sweep(rhs, weights, inverses, middle)
    targets = []
    for j in range(steps):
        t = rhs[j] + cy[j] * upper(u[j], 0) + cyl[j] * lower(u[j], 0)
        targets.append(t + cz[j] * upper(u[j], 1) + lower(cz[j], 1) * lower(u[j], 1))
    u = sweep(targets, weights, inverses, middle)

    own = (row == 1) | (row == 2)
    for j in range(0, steps, 2):
        send[j * 4 : j * 4 + TILE] = jnp.where(own, u[j], pltpu.roll(u[j + 1], 2, 0))
    for j in range(steps):
        at = slice(j * TILE, (j + 1) * TILE)
        rhs_out[at] = rhs[j]
        cy_out[at] = cy[j]
        cyl_out[at] = cyl[j]
        cz_out[at] = cz[j]
        u_out[at] = u[j]
        if j < steps - 1:
            weight_out[at] = weights[j]
            inverse_out[at] = inverses[j]
    for i in range(3):
        middle_out[i * TILE : (i + 1) * TILE] = middle[i]
    for s in range(groups):
        well_rows[s : s + 1] = received[s, WELL_ROW : WELL_ROW + 1]


def second_kernel(rhs_in, cy_in, cyl_in, cz_in, weight_in, inverse_in, middle_in, u_in, from_below, from_above, out):
    steps = rhs_in.shape[0] // TILE
    row = sublane() % 4

    def tiles(ref, count):
        return [ref[j * TILE : (j + 1) * TILE] for j in range(count)]

    rhs, cy, cyl, cz, own = (tiles(ref, steps) for ref in (rhs_in, cy_in, cyl_in, cz_in, u_in))
    weights = tiles(weight_in, steps - 1)
    inverses = tiles(inverse_in, steps - 1)
    middle = tiles(middle_in, 3)
    below = tiles(from_below, steps // 2)
    above = tiles(from_above, steps // 2)

    def turned(x, by):
        return pltpu.roll(x, by % TILE, 0) if by % TILE else x

    targets = []
    for j in range(steps):
        b, a = below[j // 2], above[j // 2]
        shift = 2 * (j % 2)
        u = jnp.where(row == 0, turned(b, -2 - shift), jnp.where(row == 3, turned(a, 2 - shift), own[j]))
        up = jnp.where(row == 3, turned(a, 1 - shift), upper(u, 0))
        down = jnp.where(row == 0, turned(b, -1 - shift), lower(u, 0))
        t = rhs[j] + cy[j] * up + cyl[j] * down
        targets.append(t + cz[j] * upper(u, 1) + lower(cz[j], 1) * lower(u, 1))
    u = sweep(targets, weights, inverses, middle)
    targets = []
    for j in range(steps):
        t = rhs[j] + cy[j] * upper(u[j], 0) + cyl[j] * lower(u[j], 0)
        targets.append(t + cz[j] * upper(u[j], 1) + lower(cz[j], 1) * lower(u[j], 1))
    u = sweep(targets, weights, inverses, middle)
    for j in range(steps):
        mirror = 2 * steps - 1 - j
        for y in range(2):
            out[y, j : j + 1] = u[j][1 + y : 2 + y]
            out[y, mirror : mirror + 1] = u[j][5 + y : 6 + y]


def call(kernel, outs, *args, scratch=(), source=pltpu.VMEM):
    return pl.pallas_call(
        kernel,
        out_shape=tuple(o if isinstance(o, jax.ShapeDtypeStruct) else jax.ShapeDtypeStruct(o, jnp.float32) for o in outs),
        in_specs=[pl.BlockSpec(memory_space=source)] * len(args),
        out_specs=tuple(pl.BlockSpec(memory_space=pltpu.VMEM) for _ in outs),
        scratch_shapes=[pltpu.VMEM(o, jnp.float32) if isinstance(o, tuple) else o for o in scratch],
        compiler_params=pltpu.CompilerParams(vmem_limit_bytes=40 << 20),
    )(*args)


def on_device(
    pressure, saturation, lam_water, lam_oil, perm_x, perm_y, perm_z, pore_volume,
    perf_cell, perf_well, well_index, well_pressure,
):
    groups = lax.axis_size("gx")
    ny = pressure.shape[1]
    wells_each = well_pressure.shape[0]
    fields = (pressure, saturation, lam_water, lam_oil, perm_x, perm_y, perm_z, pore_volume)
    given = fields + tuple(v.reshape(1, -1) for v in (perf_cell, perf_well, well_index, well_pressure))
    up = [(i, i + 1) for i in range(groups - 1)]
    down = [(i + 1, i) for i in range(groups - 1)]

    *loaded, edge = call(
        load_kernel,
        [jax.ShapeDtypeStruct(v.shape, v.dtype) for v in given] + [(5, ny, LANES)],
        *given,
        scratch=[pltpu.SemaphoreType.DMA((len(given) + 5,))],
        source=pltpu.HBM,
    )
    press, sat, lamw, lamo, permx, permy, permz, pore, cell, well, index, bhp = loaded
    from_below = lax.ppermute(edge, "gx", up)
    box = (2, ny, LANES)
    rhs, diag, cy, cz, inner, weight, well_rows = call(
        functools.partial(cell_kernel, groups),
        [box] * 4 + [(ny, LANES), (2 * ny, LANES), (groups, LANES)],
        sat, lamw, lamo, permx, permy, permz, pore, cell, well, index, bhp,
    )
    packed, sat_face = call(
        functools.partial(pack_kernel, groups),
        [(groups, CHUNK, LANES), box],
        press, sat, lamw, lamo, permx, from_below, rhs, diag, cy, cz, inner, well_rows,
        scratch=[(4, 2, ny + 2 * TILE, LANES), (3, ny + 2 * TILE, LANES)],
    )
    received = lax.all_to_all(packed, "gx", split_axis=0, concat_axis=0, tiled=True)
    partial, back = call(
        sat_kernel, [box, (ny, LANES)],
        press, sat, lamw, lamo, permx, permy, permz, pore, weight, sat_face, from_below,
    )
    from_above = lax.ppermute(back, "gx", down)

    steps = groups
    column = (steps * TILE, LANES)
    *state, send, well_rows = call(
        first_kernel,
        [column] * 6 + [(3 * TILE, LANES), column, (steps * 4, LANES), (groups, LANES)],
        received,
    )
    u_below = lax.ppermute(send, "gx", up)
    u_above = lax.ppermute(send, "gx", down)
    grad_sat, grad_bhp = call(
        well_kernel, [box, (1, wells_each)],
        partial, from_above, sat, lamw, lamo, cell, well, index, well_rows,
    )
    (columns,) = call(second_kernel, [(2, 2 * steps, LANES)], *state, u_below, u_above)
    return grad_sat, grad_bhp.reshape(wells_each), jnp.transpose(columns, (0, 2, 1))


def solution(mesh):
    cells = P(("members", "gx"), None, None)
    line = P(("members", "gx"))
    return jax.shard_map(
        on_device,
        mesh=mesh,
        in_specs=(cells,) * 8 + (line,) * 4,
        out_specs=(cells, line, cells),
        check_vma=False,
    )
```

profile of v0, /device:TPU:3, one launch (start us, length us, event | category | flops | bytes accessed | tf_op | source)
XLA Modules:
  0.0 46.4 jit_solution(12006138781836701560)
XLA Ops:
  0.6 0.0 copy-start.9
  0.6 0.0 copy-start.10
  0.7 0.0 copy-start.8
  0.7 0.0 copy-start.11
  0.7 0.6 %copy-done.9 = s32[256]{0:T(256)S(1)} copy-done((s32[256]{0:T(256)S(1)}, s32[256]{0:T(256)}, u32[]{:S(2)}) %copy-start.9) | copy-done | bytes 1048
  1.3 0.0 copy-done.10
  1.3 0.0 copy-done.8
  1.3 0.0 copy-done.11
  1.3 0.0 copy-start
  1.4 0.8 %copy-done = f32[2,32,128]{2,1,0:T(8,128)S(1)} copy-done((f32[2,32,128]{2,1,0:T(8,128)S(1)}, f32[2,32,128]{2,1,0:T(8,128)}, u32[]{:S(2)}) %copy-start) | copy-done | bytes 32792
  2.1 0.0 copy-start.1
  2.1 0.8 %copy-done.1 = f32[2,32,128]{2,1,0:T(8,128)S(1)} copy-done((f32[2,32,128]{2,1,0:T(8,128)S(1)}, f32[2,32,128]{2,1,0:T(8,128)}, u32[]{:S(2)}) %copy-start.1) | copy-done | bytes 32792
  2.9 0.0 copy-start.2
  2.9 0.8 %copy-done.2 = f32[2,32,128]{2,1,0:T(8,128)S(1)} copy-done((f32[2,32,128]{2,1,0:T(8,128)S(1)}, f32[2,32,128]{2,1,0:T(8,128)}, u32[]{:S(2)}) %copy-start.2) | copy-done | bytes 32792
  3.6 0.0 copy-start.3
  3.6 0.8 %copy-done.3 = f32[2,32,128]{2,1,0:T(8,128)S(1)} copy-done((f32[2,32,128]{2,1,0:T(8,128)S(1)}, f32[2,32,128]{2,1,0:T(8,128)}, u32[]{:S(2)}) %copy-start.3) | copy-done | bytes 32792
  4.4 0.0 copy-start.4
  4.4 0.8 %copy-done.4 = f32[2,32,128]{2,1,0:T(8,128)S(1)} copy-done((f32[2,32,128]{2,1,0:T(8,128)S(1)}, f32[2,32,128]{2,1,0:T(8,128)}, u32[]{:S(2)}) %copy-start.4) | copy-done | bytes 32792
  5.1 0.0 copy-start.5
  5.1 0.8 %copy-done.5 = f32[2,32,128]{2,1,0:T(8,128)S(1)} copy-done((f32[2,32,128]{2,1,0:T(8,128)S(1)}, f32[2,32,128]{2,1,0:T(8,128)}, u32[]{:S(2)}) %copy-start.5) | copy-done | bytes 32792
  5.9 0.0 copy-start.6
  5.9 0.8 %copy-done.6 = f32[2,32,128]{2,1,0:T(8,128)S(1)} copy-done((f32[2,32,128]{2,1,0:T(8,128)S(1)}, f32[2,32,128]{2,1,0:T(8,128)}, u32[]{:S(2)}) %copy-start.6) | copy-done | bytes 32792
  6.7 0.0 copy-start.7
  6.7 0.8 %copy-done.7 = f32[2,32,128]{2,1,0:T(8,128)S(1)} copy-done((f32[2,32,128]{2,1,0:T(8,128)S(1)}, f32[2,32,128]{2,1,0:T(8,128)}, u32[]{:S(2)}) %copy-start.7) | copy-done | bytes 32792
  7.4 0.7 %shard_map.139 = (f32[2,32,128]{2,1,0:T(8,128)S(1)}, f32[2,32,128]{2,1,0:T(8,128)S(1)}, f32[2,32,128]{2,1,0:T(8,128)S(1)}, f32[2,32,128]{2,1,0:T(8,128)S(1)}, f3...) custom-call(f32[2,32,128]{2,1,0:T(8,128)S(1)} %copy-done, ...), custom_call_target="tpu_custom_call" | custom-call | tf_op jit(solution)/shard_map/pallas_call | solution.py:367
  8.1 3.7 %collective-permute-start = (f32[5,32,128]{2,1,0:T(8,128)S(1)}, f32[5,32,128]{2,1,0:T(8,128)S(1)}, u32[]{:S(2)}, u32[]{:S(2)}) collective-permute-start(f32[5,32,128]{2,1,0:T(8,128)S(1)} %get-tuple-element.52), channel_id=1, source_target_pairs={{0,1},{1,2},{2,3},{3,4},{4,5},{5,6},{6,7},{7,8},{8,9},{9,10},{10,1... | collective-permute-start | bytes 245768 | tf_op jit(solution)/shard_map/ppermute | solution.py:397
  11.9 0.4 shard_map.140
  12.3 1.1 %collective-permute-done.from_below = f32[5,32,128]{2,1,0:T(8,128)S(1)} collective-permute-done((f32[5,32,128]{2,1,0:T(8,128)S(1)}, f32[5,32,128]{2,1,0:T(8,128)S(1)}, u32[]{:S(2)}, u32[]{:S(2)}) %collective-permute-start) | collective-permute-done | bytes 81952 | tf_op jit(solution)/shard_map/ppermute | solution.py:397
  13.3 0.1 shard_map.141
  13.4 18.1 %all_to_all.5.received = f32[16,48,128]{2,1,0:T(8,128)S(1)} all-to-all(f32[16,48,128]{2,1,0:T(8,128)S(1)} %get-tuple-element.62), channel_id=1, replica_groups=mesh['members'=2,'gx'=16] {'gx'}, dimensions={0} | all-to-all | bytes 786432 | tf_op jit(solution)/shard_map/all_to_all | solution.py:410
  31.5 0.3 shard_map.143
  31.9 1.9 %collective-permute-start.3 = (f32[64,128]{1,0:T(8,128)S(1)}, f32[64,128]{1,0:T(8,128)S(1)}, u32[]{:S(2)}, u32[]{:S(2)}) collective-permute-start(f32[64,128]{1,0:T(8,128)S(1)} %get-tuple-element.74), channel_id=1, source_target_pairs={{1,0},{2,1},{3,2},{4,3},{5,4},{6,5},{7,6},{8,7},{9,8},{10,9},{11,1... | collective-permute-start | bytes 98312 | tf_op jit(solution)/shard_map/ppermute | solution.py:425
  33.8 4.5 %collective-permute-start.2 = (f32[64,128]{1,0:T(8,128)S(1)}, f32[64,128]{1,0:T(8,128)S(1)}, u32[]{:S(2)}, u32[]{:S(2)}) collective-permute-start(f32[64,128]{1,0:T(8,128)S(1)} %get-tuple-element.74), channel_id=1, source_target_pairs={{0,1},{1,2},{2,3},{3,4},{4,5},{5,6},{6,7},{7,8},{8,9},{9,10},{10,1... | collective-permute-start | bytes 98312 | tf_op jit(solution)/shard_map/ppermute | solution.py:424
  38.3 0.2 shard_map.142
  38.5 1.9 %collective-permute-start.1 = (f32[32,128]{1,0:T(8,128)S(1)}, f32[32,128]{1,0:T(8,128)S(1)}, u32[]{:S(2)}, u32[]{:S(2)}) collective-permute-start(f32[32,128]{1,0:T(8,128)S(1)} %get-tuple-element.61), channel_id=1, source_target_pairs={{1,0},{2,1},{3,2},{4,3},{5,4},{6,5},{7,6},{8,7},{9,8},{10,9},{11,1... | collective-permute-start | bytes 49160 | tf_op jit(solution)/shard_map/ppermute | solution.py:415
  40.5 4.0 %collective-permute-done.1.from_above = f32[32,128]{1,0:T(8,128)S(1)} collective-permute-done((f32[32,128]{1,0:T(8,128)S(1)}, f32[32,128]{1,0:T(8,128)S(1)}, u32[]{:S(2)}, u32[]{:S(2)}) %collective-permute-start.1) | collective-permute-done | bytes 16416 | tf_op jit(solution)/shard_map/ppermute | solution.py:415
  44.5 1.0 %shard_map.144 = (f32[2,32,128]{2,1,0:T(8,128)}, f32[1,16]{1,0:T(1,128)}) custom-call(f32[2,32,128]{2,1,0:T(8,128)S(1)} %get-tuple-element.60.partial, f32[32,128]{1,0:T(8,128)S(1)} %collective-permute-done.1.from_above, f32[2,32,128]{2,1,0:T(8,128)S(1)} %get-tuple-element.40.sat, f32[2,32,128]{2,1,0:T(8,128)S(1)} %get-tuple-element.41.lamw, ...), custom_call_target="tpu_custom_call" | custom-call | tf_op jit(solution)/shard_map/pallas_call | solution.py:367
  45.4 0.0 collective-permute-done.3.from_above
  45.5 0.0 collective-permute-done.2.from_below
  45.5 0.9 %shard_map.145 = f32[2,32,128]{2,1,0:T(8,128)} custom-call(f32[128,128]{1,0:T(8,128)S(1)} %get-tuple-element.66.rhs_in, f32[128,128]{1,0:T(8,128)S(1)} %get-tuple-element.67.cy_in, f32[128,128]{1,0:T(8,128)S(1)} %get-tuple-element.68.cyl_in, f32[128,128]{1,0:T(8,128)S(1)} %get-tuple-element.69.cz_in, f32[128,128]{1,0:T(8,128)S(1)} %get-tuple-element.70.weight_in, ...), custom_call_target="tpu_custom_call" | custom-call | tf_op jit(solution)/shard_map/pallas_call | solution.py:367
Async XLA Ops:
  0.6 0.7 %copy-start.9 = (s32[256]{0:T(256)S(1)}, s32[256]{0:T(256)}, u32[]{:S(2)}) copy-start(s32[256]{0:T(256)} %param.21) | copy-start | bytes 3076
  0.6 0.7 %copy-start.10 = (f32[256]{0:T(256)S(1)}, f32[256]{0:T(256)}, u32[]{:S(2)}) copy-start(f32[256]{0:T(256)} %param.22) | copy-start | bytes 3076
  0.7 0.7 %copy-start.8 = (s32[256]{0:T(256)S(1)}, s32[256]{0:T(256)}, u32[]{:S(2)}) copy-start(s32[256]{0:T(256)} %param.20) | copy-start | bytes 3076
  0.7 0.7 %copy-start.11 = (f32[16]{0:T(128)S(1)}, f32[16]{0:T(128)}, u32[]{:S(2)}) copy-start(f32[16]{0:T(128)} %param.23) | copy-start | bytes 196
  1.3 0.8 %copy-start = (f32[2,32,128]{2,1,0:T(8,128)S(1)}, f32[2,32,128]{2,1,0:T(8,128)}, u32[]{:S(2)}) copy-start(f32[2,32,128]{2,1,0:T(8,128)} %refs_0_.1) | copy-start | bytes 98308
  2.1 0.8 %copy-start.1 = (f32[2,32,128]{2,1,0:T(8,128)S(1)}, f32[2,32,128]{2,1,0:T(8,128)}, u32[]{:S(2)}) copy-start(f32[2,32,128]{2,1,0:T(8,128)} %refs_1_.1) | copy-start | bytes 98308
  2.9 0.8 %copy-start.2 = (f32[2,32,128]{2,1,0:T(8,128)S(1)}, f32[2,32,128]{2,1,0:T(8,128)}, u32[]{:S(2)}) copy-start(f32[2,32,128]{2,1,0:T(8,128)} %refs_2_.1) | copy-start | bytes 98308
  3.6 0.8 %copy-start.3 = (f32[2,32,128]{2,1,0:T(8,128)S(1)}, f32[2,32,128]{2,1,0:T(8,128)}, u32[]{:S(2)}) copy-start(f32[2,32,128]{2,1,0:T(8,128)} %refs_3_.1) | copy-start | bytes 98308
  4.4 0.8 %copy-start.4 = (f32[2,32,128]{2,1,0:T(8,128)S(1)}, f32[2,32,128]{2,1,0:T(8,128)}, u32[]{:S(2)}) copy-start(f32[2,32,128]{2,1,0:T(8,128)} %refs_4_.1) | copy-start | bytes 98308
  5.1 0.8 %copy-start.5 = (f32[2,32,128]{2,1,0:T(8,128)S(1)}, f32[2,32,128]{2,1,0:T(8,128)}, u32[]{:S(2)}) copy-start(f32[2,32,128]{2,1,0:T(8,128)} %refs_5_.1) | copy-start | bytes 98308
  5.9 0.8 %copy-start.6 = (f32[2,32,128]{2,1,0:T(8,128)S(1)}, f32[2,32,128]{2,1,0:T(8,128)}, u32[]{:S(2)}) copy-start(f32[2,32,128]{2,1,0:T(8,128)} %refs_6_.1) | copy-start | bytes 98308
  6.7 0.8 %copy-start.7 = (f32[2,32,128]{2,1,0:T(8,128)S(1)}, f32[2,32,128]{2,1,0:T(8,128)}, u32[]{:S(2)}) copy-start(f32[2,32,128]{2,1,0:T(8,128)} %refs_7_.1) | copy-start | bytes 98308
  8.1 5.2 %collective-permute-start = (f32[5,32,128]{2,1,0:T(8,128)S(1)}, f32[5,32,128]{2,1,0:T(8,128)S(1)}, u32[]{:S(2)}, u32[]{:S(2)}) collective-permute-start(f32[5,32,128]{2,1,0:T(8,128)S(1)} %get-tuple-element.52), channel_id=1, source_target_pairs={{0,1},{1,2},{2,3},{3,4},{4,5},{5,6},{6,7},{7,8},{8,9},{9,10},{10,1... | collective-permute-start | bytes 245768 | tf_op jit(solution)/shard_map/ppermute | solution.py:397
  31.9 13.6 %collective-permute-start.3 = (f32[64,128]{1,0:T(8,128)S(1)}, f32[64,128]{1,0:T(8,128)S(1)}, u32[]{:S(2)}, u32[]{:S(2)}) collective-permute-start(f32[64,128]{1,0:T(8,128)S(1)} %get-tuple-element.74), channel_id=1, source_target_pairs={{1,0},{2,1},{3,2},{4,3},{5,4},{6,5},{7,6},{8,7},{9,8},{10,9},{11,1... | collective-permute-start | bytes 98312 | tf_op jit(solution)/shard_map/ppermute | solution.py:425
  33.8 11.7 %collective-permute-start.2 = (f32[64,128]{1,0:T(8,128)S(1)}, f32[64,128]{1,0:T(8,128)S(1)}, u32[]{:S(2)}, u32[]{:S(2)}) collective-permute-start(f32[64,128]{1,0:T(8,128)S(1)} %get-tuple-element.74), channel_id=1, source_target_pairs={{0,1},{1,2},{2,3},{3,4},{4,5},{5,6},{6,7},{7,8},{8,9},{9,10},{10,1... | collective-permute-start | bytes 98312 | tf_op jit(solution)/shard_map/ppermute | solution.py:424
  38.5 6.0 %collective-permute-start.1 = (f32[32,128]{1,0:T(8,128)S(1)}, f32[32,128]{1,0:T(8,128)S(1)}, u32[]{:S(2)}, u32[]{:S(2)}) collective-permute-start(f32[32,128]{1,0:T(8,128)S(1)} %get-tuple-element.61), channel_id=1, source_target_pairs={{1,0},{2,1},{3,2},{4,3},{5,4},{6,5},{7,6},{8,7},{9,8},{10,9},{11,1... | collective-permute-start | bytes 49160 | tf_op jit(solution)/shard_map/ppermute | solution.py:415
where the time goes:
time: 47.2 us; the launch traced here: 46.4 us
  blocking collectives  18.1 us (38%)
  starting transfers between devices  12.1 us (26%)
  local copies, waits for them, and re-layouts  6.74 us (14%)
  waiting for transfers between devices  5.1 us (11%)
  Pallas kernels  3.59 us (8%)
  between operations  0.74 us (2%)
    all_to_all x1, blocking collectives, on_device(): lax.all_to_all(packed, 'gx', split_axis=0, concat_axis=0, tiled=True)  18.1 us
    unnamed x24, local copies, waits for them, and re-layouts  6.74 us
    ppermute x1, starting transfers between devices, on_device(): u_below = lax.ppermute(send, 'gx', up)  4.54 us
    ppermute x1, waiting for transfers between devices, on_device(): from_above = lax.ppermute(back, 'gx', down)  4.03 us
    ppermute x1, starting transfers between devices, on_device(): from_below = lax.ppermute(edge, 'gx', up)  3.74 us
    pallas_call x7, Pallas kernels, call(): pl.pallas_call(kernel, out_shape=tuple((o if isinstance(o, jax.ShapeDtype...  3.59 us
    ppermute x1, starting transfers between devices, on_device(): from_above = lax.ppermute(back, 'gx', down)  1.92 us
    ppermute x1, starting transfers between devices, on_device(): u_above = lax.ppermute(send, 'gx', down)  1.92 us
  transfers between devices with their start and end apart: 4, of which 2 were waited for; matrix products, arithmetic and copies ran while one was open for 0% of the time, Pallas kernels for 3%

commit v1 on v0

--- a/solution.py
+++ b/solution.py
@@ -250,7 +250,7 @@
     return found[::-1]
 
 
-def first_kernel(received, rhs_out, cy_out, cyl_out, cz_out, weight_out, inverse_out, middle_out, u_out, send, well_rows):
+def first_kernel(received, _, rhs_out, cy_out, cyl_out, cz_out, weight_out, inverse_out, middle_out, u_out, send, well_rows):
     groups = received.shape[0]
     steps = groups
     low = sublane() < 4
@@ -363,14 +363,14 @@
             out[y, mirror : mirror + 1] = u[j][5 + y : 6 + y]
 
 
-def call(kernel, outs, *args, scratch=(), source=pltpu.VMEM):
+def call(kernel, outs, *args, scratch=(), source=pltpu.VMEM, limit=40 << 20):
     return pl.pallas_call(
         kernel,
         out_shape=tuple(o if isinstance(o, jax.ShapeDtypeStruct) else jax.ShapeDtypeStruct(o, jnp.float32) for o in outs),
         in_specs=[pl.BlockSpec(memory_space=source)] * len(args),
         out_specs=tuple(pl.BlockSpec(memory_space=pltpu.VMEM) for _ in outs),
         scratch_shapes=[pltpu.VMEM(o, jnp.float32) if isinstance(o, tuple) else o for o in scratch],
-        compiler_params=pltpu.CompilerParams(vmem_limit_bytes=40 << 20),
+        compiler_params=pltpu.CompilerParams(vmem_limit_bytes=limit),
     )(*args)
 
 
@@ -389,9 +389,10 @@
     *loaded, edge = call(
         load_kernel,
         [jax.ShapeDtypeStruct(v.shape, v.dtype) for v in given] + [(5, ny, LANES)],
-        *given,
+        *(pltpu.with_memory_space_constraint(v, pltpu.HBM) for v in given),
         scratch=[pltpu.SemaphoreType.DMA((len(given) + 5,))],
         source=pltpu.HBM,
+        limit=40 << 20,
     )
     press, sat, lamw, lamo, permx, permy, permz, pore, cell, well, index, bhp = loaded
     from_below = lax.ppermute(edge, "gx", up)
@@ -420,6 +421,7 @@
         first_kernel,
         [column] * 6 + [(3 * TILE, LANES), column, (steps * 4, LANES), (groups, LANES)],
         received,
+        from_above,
     )
     u_below = lax.ppermute(send, "gx", up)
     u_above = lax.ppermute(send, "gx", down)

time: 47.2 us -> 36.6 us (0.78)
  the two profiles are of different devices: /device:TPU:3 before, /device:TPU:8 now
where the time goes in v1:
time: 36.6 us; the launch traced here: 36.2 us
  starting transfers between devices  15.6 us (43%)
  waiting for transfers between devices  15.3 us (42%)
  Pallas kernels  4.74 us (13%)
  between operations  0.69 us (2%)
    all_to_all x1, waiting for transfers between devices, on_device(): lax.all_to_all(packed, 'gx', split_axis=0, concat_axis=0, tiled=True)  5.96 us
    all_to_all x1, starting transfers between devices, on_device(): lax.all_to_all(packed, 'gx', split_axis=0, concat_axis=0, tiled=True)  5.37 us
    pallas_call x7, Pallas kernels, call(): pl.pallas_call(kernel, out_shape=tuple((o if isinstance(o, jax.ShapeDtype...  4.74 us
    ppermute x1, waiting for transfers between devices, on_device(): from_below = lax.ppermute(edge, 'gx', up)  4.34 us
    ppermute x1, waiting for transfers between devices, on_device(): u_below = lax.ppermute(send, 'gx', up)  3.24 us
    ppermute x1, starting transfers between devices, on_device(): u_above = lax.ppermute(send, 'gx', down)  3.22 us
    ppermute x1, starting transfers between devices, on_device(): from_above = lax.ppermute(back, 'gx', down)  3.12 us
    ppermute x1, starting transfers between devices, on_device(): u_below = lax.ppermute(send, 'gx', up)  1.92 us
  transfers between devices with their start and end apart: 5, of which 4 were waited for; matrix products, arithmetic and copies ran while one was open for 0% of the time, Pallas kernels for 4%

profile of v1, /device:TPU:8, one launch (start us, length us, event | category | flops | bytes accessed | tf_op | source)
XLA Modules:
  0.0 36.2 jit_solution(15499918425125940074)
XLA Ops:
  0.6 1.1 %shard_map.139 = (f32[2,32,128]{2,1,0:T(8,128)S(1)}, f32[2,32,128]{2,1,0:T(8,128)S(1)}, f32[2,32,128]{2,1,0:T(8,128)S(1)}, f32[2,32,128]{2,1,0:T(8,128)S(1)}, f3...) custom-call(f32[2,32,128]{2,1,0:T(8,128)} %refs_0_.1, ...), custom_call_target="tpu_custom_call" | custom-call | tf_op jit(solution)/shard_map/pallas_call | solution.py:367
  1.8 1.9 %collective-permute-start = (f32[5,32,128]{2,1,0:T(8,128)S(1)}, f32[5,32,128]{2,1,0:T(8,128)S(1)}, u32[]{:S(2)}, u32[]{:S(2)}) collective-permute-start(f32[5,32,128]{2,1,0:T(8,128)S(1)} %get-tuple-element.52), channel_id=1, source_target_pairs={{0,1},{1,2},{2,3},{3,4},{4,5},{5,6},{6,7},{7,8},{8,9},{9,10},{10,1... | collective-permute-start | bytes 245768 | tf_op jit(solution)/shard_map/ppermute | solution.py:398
  3.7 0.4 %shard_map.140 = (f32[2,32,128]{2,1,0:T(8,128)S(1)}, f32[2,32,128]{2,1,0:T(8,128)S(1)}, f32[2,32,128]{2,1,0:T(8,128)S(1)}, f32[2,32,128]{2,1,0:T(8,128)S(1)}, f3...) custom-call(f32[2,32,128]{2,1,0:T(8,128)S(1)} %get-tuple-element.40.sat, ...), custom_call_target="tpu_custom_call" | custom-call | tf_op jit(solution)/shard_map/pallas_call | solution.py:367
  4.1 4.3 %collective-permute-done.from_below = f32[5,32,128]{2,1,0:T(8,128)S(1)} collective-permute-done((f32[5,32,128]{2,1,0:T(8,128)S(1)}, f32[5,32,128]{2,1,0:T(8,128)S(1)}, u32[]{:S(2)}, u32[]{:S(2)}) %collective-permute-start) | collective-permute-done | bytes 81952 | tf_op jit(solution)/shard_map/ppermute | solution.py:398
  8.4 0.8 %shard_map.141 = (f32[16,48,128]{2,1,0:T(8,128)}, f32[2,32,128]{2,1,0:T(8,128)S(1)}) custom-call(f32[2,32,128]{2,1,0:T(8,128)S(1)} %get-tuple-element.39.press, f32[2,32,128]{2,1,0:T(8,128)S(1)} %get-tuple-element.40.sat, f32[2,32,128]{2,1,0:T(8,128)S(1)} %get-tuple-element.41.lamw, f32[2,32,128]{2,1,0:T(8,128)S(1)} %get-tuple-element.42.lamo, ...), custom_call_target="tpu_custom_call" | custom-call | tf_op jit(solution)/shard_map/pallas_call | solution.py:367
  9.3 5.4 %all-to-all-start = ((f32[16,48,128]{2,1,0:T(8,128)}), f32[16,48,128]{2,1,0:T(8,128)S(1)}, u32[]{:S(2)}, u32[]{:S(2)}) async-start(f32[16,48,128]{2,1,0:T(8,128)} %get-tuple-element.62), calls=%async_computation | async-start | bytes 786432 | tf_op jit(solution)/shard_map/all_to_all | solution.py:411
  14.6 0.2 shard_map.142
  14.8 3.1 %collective-permute-start.1 = (f32[32,128]{1,0:T(8,128)S(1)}, f32[32,128]{1,0:T(8,128)S(1)}, u32[]{:S(2)}, u32[]{:S(2)}) collective-permute-start(f32[32,128]{1,0:T(8,128)S(1)} %get-tuple-element.61), channel_id=1, source_target_pairs={{1,0},{2,1},{3,2},{4,3},{5,4},{6,5},{7,6},{8,7},{9,8},{10,9},{11,1... | collective-permute-start | bytes 49160 | tf_op jit(solution)/shard_map/ppermute | solution.py:416
  17.9 1.7 %collective-permute-done.1._.from_above = f32[32,128]{1,0:T(8,128)S(1)} collective-permute-done((f32[32,128]{1,0:T(8,128)S(1)}, f32[32,128]{1,0:T(8,128)S(1)}, u32[]{:S(2)}, u32[]{:S(2)}) %collective-permute-start.1) | collective-permute-done | bytes 16416 | tf_op jit(solution)/shard_map/ppermute | solution.py:416
  19.7 6.0 %all-to-all-done.received = f32[16,48,128]{2,1,0:T(8,128)S(1)} async-done(((f32[16,48,128]{2,1,0:T(8,128)}), f32[16,48,128]{2,1,0:T(8,128)S(1)}, u32[]{:S(2)}, u32[]{:S(2)}) %all-to-all-start) | async-done | bytes 393248 | tf_op jit(solution)/shard_map/all_to_all | solution.py:411
  25.6 0.3 shard_map.143
  26.0 3.2 %collective-permute-start.3 = (f32[64,128]{1,0:T(8,128)S(1)}, f32[64,128]{1,0:T(8,128)S(1)}, u32[]{:S(2)}, u32[]{:S(2)}) collective-permute-start(f32[64,128]{1,0:T(8,128)S(1)} %get-tuple-element.74), channel_id=1, source_target_pairs={{1,0},{2,1},{3,2},{4,3},{5,4},{6,5},{7,6},{8,7},{9,8},{10,9},{11,1... | collective-permute-start | bytes 98312 | tf_op jit(solution)/shard_map/ppermute | solution.py:427
  29.2 1.9 %collective-permute-start.2 = (f32[64,128]{1,0:T(8,128)S(1)}, f32[64,128]{1,0:T(8,128)S(1)}, u32[]{:S(2)}, u32[]{:S(2)}) collective-permute-start(f32[64,128]{1,0:T(8,128)S(1)} %get-tuple-element.74), channel_id=1, source_target_pairs={{0,1},{1,2},{2,3},{3,4},{4,5},{5,6},{6,7},{7,8},{8,9},{9,10},{10,1... | collective-permute-start | bytes 98312 | tf_op jit(solution)/shard_map/ppermute | solution.py:426
  31.1 1.0 %shard_map.144 = (f32[2,32,128]{2,1,0:T(8,128)}, f32[1,16]{1,0:T(1,128)}) custom-call(f32[2,32,128]{2,1,0:T(8,128)S(1)} %get-tuple-element.60.partial, f32[32,128]{1,0:T(8,128)S(1)} %collective-permute-done.1._.from_above, f32[2,32,128]{2,1,0:T(8,128)S(1)} %get-tuple-element.40.sat, f32[2,32,128]{2,1,0:T(8,128)S(1)} %get-tuple-element.41.lamw, ...), custom_call_target="tpu_custom_call" | custom-call | tf_op jit(solution)/shard_map/pallas_call | solution.py:367
  32.1 0.0 collective-permute-done.3.from_above
  32.1 3.2 %collective-permute-done.2.from_below = f32[64,128]{1,0:T(8,128)S(1)} collective-permute-done((f32[64,128]{1,0:T(8,128)S(1)}, f32[64,128]{1,0:T(8,128)S(1)}, u32[]{:S(2)}, u32[]{:S(2)}) %collective-permute-start.2) | collective-permute-done | bytes 32800 | tf_op jit(solution)/shard_map/ppermute | solution.py:426
  35.3 0.9 %shard_map.145 = f32[2,32,128]{2,1,0:T(8,128)} custom-call(f32[128,128]{1,0:T(8,128)S(1)} %get-tuple-element.66.rhs_in, f32[128,128]{1,0:T(8,128)S(1)} %get-tuple-element.67.cy_in, f32[128,128]{1,0:T(8,128)S(1)} %get-tuple-element.68.cyl_in, f32[128,128]{1,0:T(8,128)S(1)} %get-tuple-element.69.cz_in, f32[128,128]{1,0:T(8,128)S(1)} %get-tuple-element.70.weight_in, ...), custom_call_target="tpu_custom_call" | custom-call | tf_op jit(solution)/shard_map/pallas_call | solution.py:367
Async XLA Ops:
  1.8 6.7 %collective-permute-start = (f32[5,32,128]{2,1,0:T(8,128)S(1)}, f32[5,32,128]{2,1,0:T(8,128)S(1)}, u32[]{:S(2)}, u32[]{:S(2)}) collective-permute-start(f32[5,32,128]{2,1,0:T(8,128)S(1)} %get-tuple-element.52), channel_id=1, source_target_pairs={{0,1},{1,2},{2,3},{3,4},{4,5},{5,6},{6,7},{7,8},{8,9},{9,10},{10,1... | collective-permute-start | bytes 245768 | tf_op jit(solution)/shard_map/ppermute | solution.py:398
  9.3 16.4 %all-to-all-start = ((f32[16,48,128]{2,1,0:T(8,128)}), f32[16,48,128]{2,1,0:T(8,128)S(1)}, u32[]{:S(2)}, u32[]{:S(2)}) async-start(f32[16,48,128]{2,1,0:T(8,128)} %get-tuple-element.62), calls=%async_computation | async-start | bytes 786432 | tf_op jit(solution)/shard_map/all_to_all | solution.py:411
  14.8 4.8 %collective-permute-start.1 = (f32[32,128]{1,0:T(8,128)S(1)}, f32[32,128]{1,0:T(8,128)S(1)}, u32[]{:S(2)}, u32[]{:S(2)}) collective-permute-start(f32[32,128]{1,0:T(8,128)S(1)} %get-tuple-element.61), channel_id=1, source_target_pairs={{1,0},{2,1},{3,2},{4,3},{5,4},{6,5},{7,6},{8,7},{9,8},{10,9},{11,1... | collective-permute-start | bytes 49160 | tf_op jit(solution)/shard_map/ppermute | solution.py:416
  26.0 6.1 %collective-permute-start.3 = (f32[64,128]{1,0:T(8,128)S(1)}, f32[64,128]{1,0:T(8,128)S(1)}, u32[]{:S(2)}, u32[]{:S(2)}) collective-permute-start(f32[64,128]{1,0:T(8,128)S(1)} %get-tuple-element.74), channel_id=1, source_target_pairs={{1,0},{2,1},{3,2},{4,3},{5,4},{6,5},{7,6},{8,7},{9,8},{10,9},{11,1... | collective-permute-start | bytes 98312 | tf_op jit(solution)/shard_map/ppermute | solution.py:427
  29.2 6.1 %collective-permute-start.2 = (f32[64,128]{1,0:T(8,128)S(1)}, f32[64,128]{1,0:T(8,128)S(1)}, u32[]{:S(2)}, u32[]{:S(2)}) collective-permute-start(f32[64,128]{1,0:T(8,128)S(1)} %get-tuple-element.74), channel_id=1, source_target_pairs={{0,1},{1,2},{2,3},{3,4},{4,5},{5,6},{6,7},{7,8},{8,9},{9,10},{10,1... | collective-permute-start | bytes 98312 | tf_op jit(solution)/shard_map/ppermute | solution.py:426
